TPU v7x, 32 devices: a whole 2x2x4 slice. The times are simulated.
32 devices in a mesh: rep: 2 (over y), seq: 4 (over x, core), head: 4 (over z).
Axes of the slice: x: 2, y: 2, z: 4, core: 2. Of those that a mesh axis runs over, the one named last changes fastest.
Arguments:
- queries: bfloat16 [2048, 4096], P(('rep', 'seq', 'head')), parts along dimension 0, may hold values from -6 to 6
- key_rows: bfloat16 [2048, 4096], P(('rep', 'seq', 'head')), parts along dimension 0, may hold values from -6 to 6
- value_rows: bfloat16 [2048, 4096], P(('rep', 'seq', 'head')), parts along dimension 0, may hold values from -6 to 6
- out_grad: bfloat16 [2048, 4096], P(('rep', 'seq', 'head')), parts along dimension 0, may hold values from -6 to 6
Outputs:
- attended: bfloat16 [2048, 4096], P(('rep', 'seq', 'head')), parts along dimension 0
- query_grad: bfloat16 [2048, 4096], P(('rep', 'seq', 'head')), parts along dimension 0
- key_grad: bfloat16 [2048, 4096], P(('rep', 'seq', 'head')), parts along dimension 0
- value_grad: bfloat16 [2048, 4096], P(('rep', 'seq', 'head')), parts along dimension 0
There are 2 independent parts, one for each index of `rep`. A program takes and returns all parts, laid end to end along the dimension named above; each array names one. Nothing has to cross between parts.
All inputs are finite; a program needn't handle non-finite values.
Results may differ from a plain program's by a relative error of at most 0.0049.
Values may be sent and summed in bfloat16 or wider, within the bound.
A program may use at most 64 MiB of HBM per device.

v0:
```python
import jax
import jax.numpy as jnp
from jax import lax
from jax.sharding import PartitionSpec as P

DH = 128
BLK_MAX = 512


def shards(queries, key_rows, value_rows, out_grad):
    f32 = jnp.float32
    bf16 = jnp.bfloat16
    head_count = lax.axis_size("head")
    tok_count = queries.shape[0]
    local_heads = queries.shape[1] // (head_count * DH)
    seq_rows = tok_count * head_count
    block = min(BLK_MAX, seq_rows)
    block_count = seq_rows // block
    factor = float(DH * seq_rows * lax.axis_size("seq")) ** (-0.5)

    def to_heads(matrix):
        return matrix.reshape(tok_count, head_count, local_heads, DH)

    def per_head(parts):
        heads_here = parts[0].shape[2]
        query_blocks, key_blocks, value_blocks, grad_blocks = (
            item.reshape(block_count, block, heads_here, DH) for item in parts
        )
        kv_state = jnp.einsum(
            "bthd,bthe->bhde", key_blocks, value_blocks, preferred_element_type=f32
        )
        grad_state = jnp.einsum(
            "bthd,bthe->bhde", query_blocks, grad_blocks, preferred_element_type=f32
        )
        empty_state = jnp.zeros((1, heads_here, DH, DH), f32)
        local_prefix = jnp.concatenate([empty_state, jnp.cumsum(kv_state, 0)[:-1]], 0)
        tail_sums = jnp.cumsum(grad_state[::-1], 0)[::-1]
        local_suffix = jnp.concatenate([tail_sums[1:], empty_state], 0)
        kv_total = jnp.sum(kv_state, 0)
        grad_total = jnp.sum(grad_state, 0)
        my_index = lax.axis_index("seq")
        pieces = (
            lax.all_gather(kv_total[None], "seq", axis=0, tiled=True),
            lax.all_gather(grad_total[None], "seq", axis=0, tiled=True),
        )
        count = pieces[0].shape[0]
        index = jnp.arange(count, dtype=jnp.int32)
        below_me = (index < my_index).astype(f32)[:, None, None, None]
        above_me = (index > my_index).astype(f32)[:, None, None, None]
        span_prefix = jnp.sum(pieces[0] * below_me, 0)
        span_suffix = jnp.sum(pieces[1] * above_me, 0)
        prefix = (local_prefix + span_prefix[None]).astype(bf16)
        suffix = (local_suffix + span_suffix[None]).astype(bf16)
        causal = (jnp.arange(block)[:, None] >= jnp.arange(block)[None, :])[None, None]
        scores = jnp.einsum("bthd,bshd->bhts", query_blocks, key_blocks, preferred_element_type=f32)
        scores = jnp.where(causal, scores * factor, 0.0).astype(bf16)
        attended = jnp.einsum("bhts,bshd->bthd", scores, value_blocks, preferred_element_type=f32)
        attended = attended + factor * jnp.einsum(
            "bthd,bhde->bthe", query_blocks, prefix, preferred_element_type=f32
        )
        dscores = jnp.einsum(
            "bthe,bshe->bhts", grad_blocks, value_blocks, preferred_element_type=f32
        )
        dscores = jnp.where(causal, dscores * factor, 0.0).astype(bf16)
        query_grad = jnp.einsum("bhts,bshd->bthd", dscores, key_blocks, preferred_element_type=f32)
        query_grad = query_grad + factor * jnp.einsum(
            "bthe,bhde->bthd", grad_blocks, prefix, preferred_element_type=f32
        )
        key_grad = jnp.einsum("bhts,bthd->bshd", dscores, query_blocks, preferred_element_type=f32)
        key_grad = key_grad + factor * jnp.einsum(
            "bshe,bhde->bshd", value_blocks, suffix, preferred_element_type=f32
        )
        value_grad = jnp.einsum("bhts,bthe->bshe", scores, grad_blocks, preferred_element_type=f32)
        value_grad = value_grad + factor * jnp.einsum(
            "bshd,bhde->bshe", key_blocks, suffix, preferred_element_type=f32
        )
        results = tuple(
            (
                item.astype(bf16).reshape(seq_rows, 1, heads_here, DH)
                for item in (attended, query_grad, key_grad, value_grad)
            )
        )
        return (
            lax.all_to_all(results[0], "head", split_axis=0, concat_axis=1, tiled=True),
            lax.all_to_all(results[1], "head", split_axis=0, concat_axis=1, tiled=True),
            lax.all_to_all(results[2], "head", split_axis=0, concat_axis=1, tiled=True),
            lax.all_to_all(results[3], "head", split_axis=0, concat_axis=1, tiled=True),
        )

    outputs = per_head(
        (
            lax.all_to_all(to_heads(queries), "head", split_axis=1, concat_axis=0, tiled=True),
            lax.all_to_all(to_heads(key_rows), "head", split_axis=1, concat_axis=0, tiled=True),
            lax.all_to_all(to_heads(value_rows), "head", split_axis=1, concat_axis=0, tiled=True),
            lax.all_to_all(to_heads(out_grad), "head", split_axis=1, concat_axis=0, tiled=True),
        )
    )
    return tuple((item.reshape(tok_count, queries.shape[1]) for item in outputs))


def solution(mesh):
    placed = (
        P(("rep", "seq", "head"), None),
        P(("rep", "seq", "head"), None),
        P(("rep", "seq", "head"), None),
        P(("rep", "seq", "head"), None),
    )
    return jax.shard_map(
        shards,
        mesh=mesh,
        in_specs=placed,
        out_specs=(
            P(("rep", "seq", "head"), None),
            P(("rep", "seq", "head"), None),
            P(("rep", "seq", "head"), None),
            P(("rep", "seq", "head"), None),
        ),
        check_vma=False,
    )
```

profile of v0, /device:TPU:0, one launch (start us, length us, event | category | flops | bytes accessed | tf_op | source)
XLA Modules:
  0.0 174.0 jit_solution(1147366358603336593)
XLA Ops:
  7.2 0.0 copy-start.4
  7.2 1.2 copy.85
  8.4 1.0 copy.50
  9.4 6.3 %all-to-all-start.1 = ((bf16[64,4,8,128]{3,0,2,1:T(8,128)(2,1)}), bf16[64,4,8,128]{3,0,2,1:T(8,128)(2,1)S(1)}, u32[]{:S(2)}, u32[]{:S(2)}) async-start(bf16[64,4,8,128]{3,0,2,1:T(8,128)(2,1)} %copy.50), calls=%async_computation.1 | async-start | bytes 1048576 | tf_op jit(solution)/shard_map/all_to_all | solution.py:93
  15.7 0.0 copy-done.4
  15.7 0.1 copy.86
  15.8 1.0 copy.52
  16.8 13.4 %all-to-all-done.1 = bf16[64,4,8,128]{3,0,2,1:T(8,128)(2,1)S(1)} async-done(((bf16[64,4,8,128]{3,0,2,1:T(8,128)(2,1)}), bf16[64,4,8,128]{3,0,2,1:T(8,128)(2,1)S(1)}, u32[]{:S(2)}, u32[]{:S(2)}) %all-to-all-start.1) | async-done | bytes 524320 | tf_op jit(solution)/shard_map/all_to_all | solution.py:93
  30.2 3.5 %all-to-all-start.2 = ((bf16[64,4,8,128]{3,0,2,1:T(8,128)(2,1)}), bf16[64,4,8,128]{3,0,2,1:T(8,128)(2,1)S(1)}, u32[]{:S(2)}, u32[]{:S(2)}) async-start(bf16[64,4,8,128]{3,0,2,1:T(8,128)(2,1)} %copy.52), calls=%async_computation.2 | async-start | bytes 1048576 | tf_op jit(solution)/shard_map/all_to_all | solution.py:94
  33.7 0.0 all-gather.5.cloned.1.call-start
  33.7 0.0 copy-start.5
  33.8 13.9 %all-to-all-done.2 = bf16[64,4,8,128]{3,0,2,1:T(8,128)(2,1)S(1)} async-done(((bf16[64,4,8,128]{3,0,2,1:T(8,128)(2,1)}), bf16[64,4,8,128]{3,0,2,1:T(8,128)(2,1)S(1)}, u32[]{:S(2)}, u32[]{:S(2)}) %all-to-all-start.2) | async-done | bytes 524320 | tf_op jit(solution)/shard_map/all_to_all | solution.py:94
  47.7 1.1 fusion.16
  48.8 0.0 all-gather.5.cloned.1.call-update
  48.8 0.0 copy-done.5
  48.8 0.1 copy.84
  48.9 1.0 copy.48
  49.9 3.5 %all-to-all-start = ((bf16[64,4,8,128]{3,0,2,1:T(8,128)(2,1)}), bf16[64,4,8,128]{3,0,2,1:T(8,128)(2,1)S(1)}, u32[]{:S(2)}, u32[]{:S(2)}) async-start(bf16[64,4,8,128]{3,0,2,1:T(8,128)(2,1)} %copy.48), calls=%async_computation | async-start | bytes 1048576 | tf_op jit(solution)/shard_map/all_to_all | solution.py:92
  53.4 0.0 copy-done.6
  53.4 0.1 copy.87
  53.5 1.0 copy.59
  54.5 12.8 %all-to-all-done = bf16[64,4,8,128]{3,0,2,1:T(8,128)(2,1)S(1)} async-done(((bf16[64,4,8,128]{3,0,2,1:T(8,128)(2,1)}), bf16[64,4,8,128]{3,0,2,1:T(8,128)(2,1)S(1)}, u32[]{:S(2)}, u32[]{:S(2)}) %all-to-all-start) | async-done | bytes 524320 | tf_op jit(solution)/shard_map/all_to_all | solution.py:92
  67.4 3.5 %all-to-all-start.4 = ((bf16[64,4,8,128]{3,0,2,1:T(8,128)(2,1)}), bf16[64,4,8,128]{3,0,2,1:T(8,128)(2,1)S(1)}, u32[]{:S(2)}, u32[]{:S(2)}) async-start(bf16[64,4,8,128]{3,0,2,1:T(8,128)(2,1)} %copy.59), calls=%async_computation.4 | async-start | bytes 1048576 | tf_op jit(solution)/shard_map/all_to_all | solution.py:95
  70.8 0.0 all-gather.7.cloned.1.call-start
  70.9 13.9 %all-to-all-done.4 = bf16[64,4,8,128]{3,0,2,1:T(8,128)(2,1)S(1)} async-done(((bf16[64,4,8,128]{3,0,2,1:T(8,128)(2,1)}), bf16[64,4,8,128]{3,0,2,1:T(8,128)(2,1)S(1)}, u32[]{:S(2)}, u32[]{:S(2)}) %all-to-all-start.4) | async-done | bytes 524320 | tf_op jit(solution)/shard_map/all_to_all | solution.py:95
  84.8 1.1 fusion.17
  86.0 0.0 all-gather.7.cloned.1.call-update
  86.1 0.4 select_convert_fusion.1
  86.5 1.4 convolution_bitcast_fusion.3
  87.9 1.9 %multiply_reduce_fusion.1 = bf16[8,128,128]{2,1,0:T(8,128)(2,1)S(1)} fusion(f32[4,8,128,128]{3,2,1,0:T(8,128)} %bitcast.130, f32[4]{0:T(128)S(1)} %compare_convert_fusion.1), kind=kLoop, calls=%fused_computation.2 | loop fusion | flops 917504 | bytes 2359312 | tf_op jit(solution)/shard_map/reduce_sum | solution.py:50
  89.9 0.0 copy-done.1
  89.9 0.3 fusion.9
  90.2 1.1 copy.57
  91.3 4.1 %all-to-all-start.3 = ((bf16[256,1,8,128]{3,2,1,0:T(8,128)(2,1)}), bf16[256,1,8,128]{3,2,1,0:T(8,128)(2,1)}, u32[]{:S(2)}, u32[]{:S(2)}) async-start(bf16[256,1,8,128]{3,2,1,0:T(8,128)(2,1)} %copy.57), calls=%async_computation.3 | async-start | bytes 1048576 | tf_op jit(solution)/shard_map/all_to_all | solution.py:84
  95.5 1.5 convolution_bitcast_fusion
  96.9 10.9 %all-gather.7.cloned.1.call-done = f32[32,128,128]{2,1,0:T(8,128)} async-done(((f32[8,128,128]{2,1,0:T(8,128)}), f32[32,128,128]{2,1,0:T(8,128)}) %all-gather.7.cloned.1.call-update) | async-done | bytes 2097168 | tf_op jit(solution)/shard_map/all_gather | solution.py:44
  107.9 1.9 %multiply_reduce_fusion = bf16[8,128,128]{2,1,0:T(8,128)(2,1)S(1)} fusion(f32[4,8,128,128]{3,2,1,0:T(8,128)} %bitcast.131, f32[4]{0:T(128)S(1)} %compare_convert_fusion), kind=kLoop, calls=%fused_computation | loop fusion | flops 917504 | bytes 2359312 | tf_op jit(solution)/shard_map/reduce_sum | solution.py:51
  109.7 0.0 copy-start.2
  109.7 0.3 fusion.8
  110.0 0.4 copy-done.2
  110.4 1.1 copy.72
  111.6 0.0 all-to-all-done.3
  111.6 4.6 %all-to-all-start.7 = ((bf16[256,1,8,128]{3,2,1,0:T(8,128)(2,1)}), bf16[256,1,8,128]{3,2,1,0:T(8,128)(2,1)}, u32[]{:S(2)}, u32[]{:S(2)}) async-start(bf16[256,1,8,128]{3,2,1,0:T(8,128)(2,1)} %copy.72), calls=%async_computation.7 | async-start | bytes 1048576 | tf_op jit(solution)/shard_map/all_to_all | solution.py:87
  116.2 0.4 select_convert_fusion
  116.6 0.5 convolution_bitcast_fusion.1
  117.1 0.0 copy-done.3
  117.1 0.3 fusion.10
  117.4 1.1 copy.67
  118.6 12.6 %all-to-all-done.7 = bf16[256,1,8,128]{3,2,1,0:T(8,128)(2,1)} async-done(((bf16[256,1,8,128]{3,2,1,0:T(8,128)(2,1)}), bf16[256,1,8,128]{3,2,1,0:T(8,128)(2,1)}, u32[]{:S(2)}, u32[]{:S(2)}) %all-to-all-start.7) | async-done | bytes 524320 | tf_op jit(solution)/shard_map/all_to_all | solution.py:87
  131.2 3.5 %all-to-all-start.6 = ((bf16[256,1,8,128]{3,2,1,0:T(8,128)(2,1)}), bf16[256,1,8,128]{3,2,1,0:T(8,128)(2,1)S(1)}, u32[]{:S(2)}, u32[]{:S(2)}) async-start(bf16[256,1,8,128]{3,2,1,0:T(8,128)(2,1)} %copy.67), calls=%async_computation.6 | async-start | bytes 1048576 | tf_op jit(solution)/shard_map/all_to_all | solution.py:86
  134.6 0.4 convolution_bitcast_fusion.2
  135.1 0.3 fusion.11
  135.4 1.1 copy.62
  136.5 12.1 %all-to-all-done.6 = bf16[256,1,8,128]{3,2,1,0:T(8,128)(2,1)S(1)} async-done(((bf16[256,1,8,128]{3,2,1,0:T(8,128)(2,1)}), bf16[256,1,8,128]{3,2,1,0:T(8,128)(2,1)S(1)}, u32[]{:S(2)}, u32[]{:S(2)}) %all-to-all-start.6) | async-done | bytes 524320 | tf_op jit(solution)/shard_map/all_to_all | solution.py:86
  148.7 3.5 %all-to-all-start.5 = ((bf16[256,1,8,128]{3,2,1,0:T(8,128)(2,1)}), bf16[256,1,8,128]{3,2,1,0:T(8,128)(2,1)S(1)}, u32[]{:S(2)}, u32[]{:S(2)}) async-start(bf16[256,1,8,128]{3,2,1,0:T(8,128)(2,1)} %copy.62), calls=%async_computation.5 | async-start | bytes 1048576 | tf_op jit(solution)/shard_map/all_to_all | solution.py:85
  152.1 1.1 copy.58
  153.3 1.0 reshape.189
  154.3 1.1 copy.73
  155.4 1.0 reshape.197
  156.4 0.1 copy.68
  156.5 1.0 reshape.195
  157.6 8.5 %all-to-all-done.5 = bf16[256,1,8,128]{3,2,1,0:T(8,128)(2,1)S(1)} async-done(((bf16[256,1,8,128]{3,2,1,0:T(8,128)(2,1)}), bf16[256,1,8,128]{3,2,1,0:T(8,128)(2,1)S(1)}, u32[]{:S(2)}, u32[]{:S(2)}) %all-to-all-start.5) | async-done | bytes 524320 | tf_op jit(solution)/shard_map/all_to_all | solution.py:85
  166.1 0.1 copy.63
  166.2 1.0 reshape.193
  (13 shorter events, 0.2 us)
Async XLA Ops:
  7.2 8.5 %copy-start.4 = (bf16[64,4096]{1,0:T(8,128)(2,1)S(1)}, bf16[64,4096]{1,0:T(8,128)(2,1)}, u32[]{:S(2)}) copy-start(bf16[64,4096]{1,0:T(8,128)(2,1)} %param.6) | copy-start | bytes 1572868
  9.4 20.8 %all-to-all-start.1 = ((bf16[64,4,8,128]{3,0,2,1:T(8,128)(2,1)}), bf16[64,4,8,128]{3,0,2,1:T(8,128)(2,1)S(1)}, u32[]{:S(2)}, u32[]{:S(2)}) async-start(bf16[64,4,8,128]{3,0,2,1:T(8,128)(2,1)} %copy.50), calls=%async_computation.1 | async-start | bytes 1048576 | tf_op jit(solution)/shard_map/all_to_all | solution.py:93
  30.2 17.4 %all-to-all-start.2 = ((bf16[64,4,8,128]{3,0,2,1:T(8,128)(2,1)}), bf16[64,4,8,128]{3,0,2,1:T(8,128)(2,1)S(1)}, u32[]{:S(2)}, u32[]{:S(2)}) async-start(bf16[64,4,8,128]{3,0,2,1:T(8,128)(2,1)} %copy.52), calls=%async_computation.2 | async-start | bytes 1048576 | tf_op jit(solution)/shard_map/all_to_all | solution.py:94
  33.7 54.2 %all-gather.5.cloned.1.call-start = ((), (), s32[]{:S(2)}) async-start(), calls=%async_computation.8 | async-start | bytes 2621440 | tf_op jit(solution)/shard_map/all_gather | solution.py:43
  33.7 15.1 %copy-start.5 = (bf16[64,4096]{1,0:T(8,128)(2,1)S(1)}, bf16[64,4096]{1,0:T(8,128)(2,1)}, u32[]{:S(2)}) copy-start(bf16[64,4096]{1,0:T(8,128)(2,1)} %param.4) | copy-start | bytes 1572868
  48.8 4.6 %copy-start.6 = (bf16[64,4096]{1,0:T(8,128)(2,1)S(1)}, bf16[64,4096]{1,0:T(8,128)(2,1)}, u32[]{:S(2)}) copy-start(bf16[64,4096]{1,0:T(8,128)(2,1)} %param.7) | copy-start | bytes 1572868
  49.9 17.4 %all-to-all-start = ((bf16[64,4,8,128]{3,0,2,1:T(8,128)(2,1)}), bf16[64,4,8,128]{3,0,2,1:T(8,128)(2,1)S(1)}, u32[]{:S(2)}, u32[]{:S(2)}) async-start(bf16[64,4,8,128]{3,0,2,1:T(8,128)(2,1)} %copy.48), calls=%async_computation | async-start | bytes 1048576 | tf_op jit(solution)/shard_map/all_to_all | solution.py:92
  67.4 17.4 %all-to-all-start.4 = ((bf16[64,4,8,128]{3,0,2,1:T(8,128)(2,1)}), bf16[64,4,8,128]{3,0,2,1:T(8,128)(2,1)S(1)}, u32[]{:S(2)}, u32[]{:S(2)}) async-start(bf16[64,4,8,128]{3,0,2,1:T(8,128)(2,1)} %copy.59), calls=%async_computation.4 | async-start | bytes 1048576 | tf_op jit(solution)/shard_map/all_to_all | solution.py:95
  70.8 37.0 %all-gather.7.cloned.1.call-start = ((), (), s32[]{:S(2)}) async-start(), calls=%async_computation.9 | async-start | bytes 2621440 | tf_op jit(solution)/shard_map/all_gather | solution.py:44
  87.9 1.9 %copy-start.1 = (f32[8,128,256]{1,2,0:T(8,128)S(1)}, f32[8,128,256]{1,2,0:T(8,128)}, u32[]{:S(2)}) copy-start(f32[8,128,256]{1,2,0:T(8,128)} %convolution_bitcast_fusion.3) | copy-start | bytes 3145732
  91.3 20.3 %all-to-all-start.3 = ((bf16[256,1,8,128]{3,2,1,0:T(8,128)(2,1)}), bf16[256,1,8,128]{3,2,1,0:T(8,128)(2,1)}, u32[]{:S(2)}, u32[]{:S(2)}) async-start(bf16[256,1,8,128]{3,2,1,0:T(8,128)(2,1)} %copy.57), calls=%async_computation.3 | async-start | bytes 1048576 | tf_op jit(solution)/shard_map/all_to_all | solution.py:84
  96.9 12.8 %copy-start = (f32[8,128,256]{1,2,0:T(8,128)S(1)}, f32[8,128,256]{1,2,0:T(8,128)}, u32[]{:S(2)}) copy-start(f32[8,128,256]{1,2,0:T(8,128)} %convolution_bitcast_fusion) | copy-start | bytes 3145732
  109.7 0.7 copy-start.2
  111.6 19.6 %all-to-all-start.7 = ((bf16[256,1,8,128]{3,2,1,0:T(8,128)(2,1)}), bf16[256,1,8,128]{3,2,1,0:T(8,128)(2,1)}, u32[]{:S(2)}, u32[]{:S(2)}) async-start(bf16[256,1,8,128]{3,2,1,0:T(8,128)(2,1)} %copy.72), calls=%async_computation.7 | async-start | bytes 1048576 | tf_op jit(solution)/shard_map/all_to_all | solution.py:87
  116.2 0.9 copy-start.3
  131.2 17.5 %all-to-all-start.6 = ((bf16[256,1,8,128]{3,2,1,0:T(8,128)(2,1)}), bf16[256,1,8,128]{3,2,1,0:T(8,128)(2,1)S(1)}, u32[]{:S(2)}, u32[]{:S(2)}) async-start(bf16[256,1,8,128]{3,2,1,0:T(8,128)(2,1)} %copy.67), calls=%async_computation.6 | async-start | bytes 1048576 | tf_op jit(solution)/shard_map/all_to_all | solution.py:86
  148.7 17.4 %all-to-all-start.5 = ((bf16[256,1,8,128]{3,2,1,0:T(8,128)(2,1)}), bf16[256,1,8,128]{3,2,1,0:T(8,128)(2,1)S(1)}, u32[]{:S(2)}, u32[]{:S(2)}) async-start(bf16[256,1,8,128]{3,2,1,0:T(8,128)(2,1)} %copy.62), calls=%async_computation.5 | async-start | bytes 1048576 | tf_op jit(solution)/shard_map/all_to_all | solution.py:85
Sparse Core Ops, SparseCore 0:
  49.0 21.6 all-gather.4
  86.1 21.6 all-gather.6
where the time goes:
time: 175 us; the launch traced here: 174 us
  waiting for transfers between devices  98.2 us (56%)
  starting transfers between devices  32.5 us (19%)
  local copies, waits for them, and re-layouts  17.1 us (10%)
  between operations  14.3 us (8%)
  matrix products  8.12 us (5%)
  other arithmetic  3.83 us (2%)
    all_to_all x1, waiting for transfers between devices, shards(): lax.all_to_all(to_heads(value_rows), 'head', split_axis=1, concat_axis=0,...  13.9 us
    all_to_all x1, waiting for transfers between devices, shards(): lax.all_to_all(to_heads(out_grad), 'head', split_axis=1, concat_axis=0, t...  13.9 us
    all_to_all x1, waiting for transfers between devices, shards(): lax.all_to_all(to_heads(key_rows), 'head', split_axis=1, concat_axis=0, t...  13.4 us
    all_to_all x1, waiting for transfers between devices, shards(): lax.all_to_all(to_heads(queries), 'head', split_axis=1, concat_axis=0, ti...  12.8 us
    all_to_all x1, waiting for transfers between devices, per_head(): lax.all_to_all(results[3], 'head', split_axis=0, concat_axis=1, tiled=True)  12.6 us
    all_to_all x1, waiting for transfers between devices, per_head(): lax.all_to_all(results[2], 'head', split_axis=0, concat_axis=1, tiled=True)  12.1 us
    all_gather x1, waiting for transfers between devices, per_head(): lax.all_gather(grad_total[None], 'seq', axis=0, tiled=True)  10.9 us
    all_to_all x1, waiting for transfers between devices, per_head(): lax.all_to_all(results[1], 'head', split_axis=0, concat_axis=1, tiled=True)  8.53 us
  transfers between devices with their start and end apart: 10, of which 8 were waited for; matrix products, arithmetic and copies ran while one was open for 14% of the time, Pallas kernels for 0%

commit v1 on v0

--- a/solution.py
+++ b/solution.py
@@ -1,3 +1,4 @@
+import functools
 import jax
 import jax.numpy as jnp
 from jax import lax
@@ -5,6 +6,27 @@
 
 DH = 128
 BLK_MAX = 512
+
+
+def cut_the_levels_all(u, bus_axis):
+    mid_arr = lax.psum(1, axis_name=bus_axis)
+    z_new = lax.axis_index(bus_axis)
+    state_next, p_next = (mid_arr, z_new)
+    base_arr = u.shape[1] // state_next
+    u1 = jnp.roll(u, shift=-p_next * base_arr, axis=1)
+    odd = lax.slice_in_dim(u1, 0, base_arr, axis=1)
+    column = [odd]
+    for b in [*range(1, state_next)]:
+        t1 = lax.slice_in_dim(u1, b * base_arr, (b + 1) * base_arr, axis=1)
+        z1 = lax.ppermute(
+            t1, axis_name=bus_axis, perm=[(it, (it + b) % state_next) for it in range(state_next)]
+        )
+        column.append(z1)
+    response = jnp.concatenate(column[::-1], axis=0)
+    return jnp.roll(response, shift=(p_next + 1) * column[0].shape[0], axis=0)
+
+
+_convert_tables = functools.partial(cut_the_levels_all, bus_axis="head")
 
 
 def shards(queries, key_rows, value_rows, out_grad):
@@ -92,7 +114,7 @@
             lax.all_to_all(to_heads(queries), "head", split_axis=1, concat_axis=0, tiled=True),
             lax.all_to_all(to_heads(key_rows), "head", split_axis=1, concat_axis=0, tiled=True),
             lax.all_to_all(to_heads(value_rows), "head", split_axis=1, concat_axis=0, tiled=True),
-            lax.all_to_all(to_heads(out_grad), "head", split_axis=1, concat_axis=0, tiled=True),
+            _convert_tables(to_heads(out_grad)),
         )
     )
     return tuple((item.reshape(tok_count, queries.shape[1]) for item in outputs))

time: 175 us -> 161 us (0.920)
  waiting for transfers between devices: 98.2 us -> 80.7 us
  matrix products: 8.12 us -> 10.7 us
    all_to_all x1 -> x0, waiting for transfers between devices: 13.9 us -> none  [shards(): lax.all_to_all(to_heads(out_grad), 'head', split_axis=1, concat_axis=0, t...]
    ppermute x0 -> x3, waiting for transfers between devices: none -> 12.1 us  [cut_the_levels_all(): lax.ppermute(t1, axis_name=bus_axis, perm=[(it, (it + b) % state_next) fo...]
    all_to_all x1, waiting for transfers between devices: 0.01 us -> 11 us  [per_head(): lax.all_to_all(results[0], 'head', split_axis=0, concat_axis=1, tiled=True)]
    all_to_all x1, waiting for transfers between devices: 12.8 us -> 1.93 us  [shards(): lax.all_to_all(to_heads(queries), 'head', split_axis=1, concat_axis=0, ti...]
    all_gather x1, waiting for transfers between devices: 10.9 us -> 0.01 us  [per_head(): lax.all_gather(grad_total[None], 'seq', axis=0, tiled=True)]
    ppermute x0 -> x3, starting transfers between devices: none -> 3.48 us  [cut_the_levels_all(): lax.ppermute(t1, axis_name=bus_axis, perm=[(it, (it + b) % state_next) fo...]
    all_to_all x1 -> x0, starting transfers between devices: 3.47 us -> none  [shards(): lax.all_to_all(to_heads(out_grad), 'head', split_axis=1, concat_axis=0, t...]
    all_to_all x1, waiting for transfers between devices: 12.6 us -> 9.56 us  [per_head(): lax.all_to_all(results[3], 'head', split_axis=0, concat_axis=1, tiled=True)]
  transfers between devices with their start and end apart: 10 -> 12, of which waited for: 8 -> 9; matrix products, arithmetic and copies ran while one was open for 14% -> 17% of each run, Pallas kernels for 0% -> 0%
where the time goes in v1:
time: 161 us; the launch traced here: 160 us
  waiting for transfers between devices  80.7 us (50%)
  starting transfers between devices  32.9 us (20%)
  local copies, waits for them, and re-layouts  16.9 us (10%)
  between operations  14.4 us (9%)
  matrix products  10.7 us (7%)
  other arithmetic  4.12 us (3%)
    all_to_all x1, waiting for transfers between devices, shards(): lax.all_to_all(to_heads(value_rows), 'head', split_axis=1, concat_axis=0,...  13.9 us
    all_to_all x1, waiting for transfers between devices, shards(): lax.all_to_all(to_heads(key_rows), 'head', split_axis=1, concat_axis=0, t...  13.4 us
    ppermute x3, waiting for transfers between devices, cut_the_levels_all(): lax.ppermute(t1, axis_name=bus_axis, perm=[(it, (it + b) % state_next) fo...  12.1 us
    all_to_all x1, waiting for transfers between devices, per_head(): lax.all_to_all(results[0], 'head', split_axis=0, concat_axis=1, tiled=True)  11 us
    all_to_all x1, waiting for transfers between devices, per_head(): lax.all_to_all(results[2], 'head', split_axis=0, concat_axis=1, tiled=True)  11 us
    all_to_all x1, waiting for transfers between devices, per_head(): lax.all_to_all(results[3], 'head', split_axis=0, concat_axis=1, tiled=True)  9.56 us
    all_to_all x1, waiting for transfers between devices, per_head(): lax.all_to_all(results[1], 'head', split_axis=0, concat_axis=1, tiled=True)  7.98 us
    all_to_all x1, starting transfers between devices, shards(): lax.all_to_all(to_heads(key_rows), 'head', split_axis=1, concat_axis=0, t...  6.32 us
  transfers between devices with their start and end apart: 12, of which 9 were waited for; matrix products, arithmetic and copies ran while one was open for 17% of the time, Pallas kernels for 0%

profile of v1, /device:TPU:0, one launch (start us, length us, event | category | flops | bytes accessed | tf_op | source)
XLA Modules:
  0.0 159.8 jit_solution(10058954697166340036)
XLA Ops:
  7.2 1.2 copy.121
  8.4 1.0 copy.83
  9.4 6.3 %all-to-all-start.1 = ((bf16[64,4,8,128]{3,0,2,1:T(8,128)(2,1)}), bf16[64,4,8,128]{3,0,2,1:T(8,128)(2,1)S(1)}, u32[]{:S(2)}, u32[]{:S(2)}) async-start(bf16[64,4,8,128]{3,0,2,1:T(8,128)(2,1)} %copy.83), calls=%async_computation.1 | async-start | bytes 1048576 | tf_op jit(solution)/shard_map/all_to_all | solution.py:115
  15.7 0.1 copy.122
  15.8 1.0 copy.85
  16.8 13.4 %all-to-all-done.1 = bf16[64,4,8,128]{3,0,2,1:T(8,128)(2,1)S(1)} async-done(((bf16[64,4,8,128]{3,0,2,1:T(8,128)(2,1)}), bf16[64,4,8,128]{3,0,2,1:T(8,128)(2,1)S(1)}, u32[]{:S(2)}, u32[]{:S(2)}) %all-to-all-start.1) | async-done | bytes 524320 | tf_op jit(solution)/shard_map/all_to_all | solution.py:115
  30.2 3.5 %all-to-all-start.2 = ((bf16[64,4,8,128]{3,0,2,1:T(8,128)(2,1)}), bf16[64,4,8,128]{3,0,2,1:T(8,128)(2,1)S(1)}, u32[]{:S(2)}, u32[]{:S(2)}) async-start(bf16[64,4,8,128]{3,0,2,1:T(8,128)(2,1)} %copy.85), calls=%async_computation.2 | async-start | bytes 1048576 | tf_op jit(solution)/shard_map/all_to_all | solution.py:116
  33.7 0.0 all-gather.5.cloned.1.call-start
  33.7 0.0 copy-start.6
  33.8 13.9 %all-to-all-done.2 = bf16[64,4,8,128]{3,0,2,1:T(8,128)(2,1)S(1)} async-done(((bf16[64,4,8,128]{3,0,2,1:T(8,128)(2,1)}), bf16[64,4,8,128]{3,0,2,1:T(8,128)(2,1)S(1)}, u32[]{:S(2)}, u32[]{:S(2)}) %all-to-all-start.2) | async-done | bytes 524320 | tf_op jit(solution)/shard_map/all_to_all | solution.py:116
  47.7 1.1 fusion.29
  48.8 0.0 all-gather.5.cloned.1.call-update
  48.8 0.0 copy-start.7
  48.9 0.1 copy.123
  49.0 0.2 copy.92
  49.2 0.2 fusion.11
  49.4 0.7 fusion.28
  50.1 1.5 collective-permute-start
  51.6 0.0 collective-permute-start.1
  51.6 0.0 copy-done.7
  51.6 0.1 copy.120
  51.7 1.0 copy.81
  52.7 4.2 %all-to-all-start = ((bf16[64,4,8,128]{3,0,2,1:T(8,128)(2,1)}), bf16[64,4,8,128]{3,0,2,1:T(8,128)(2,1)S(1)}, u32[]{:S(2)}, u32[]{:S(2)}) async-start(bf16[64,4,8,128]{3,0,2,1:T(8,128)(2,1)} %copy.81), calls=%async_computation | async-start | bytes 1048576 | tf_op jit(solution)/shard_map/all_to_all | solution.py:114
  56.9 2.0 %collective-permute-start.2 = (bf16[64,1,8,128]{3,0,2,1:T(8,128)(2,1)}, bf16[64,1,8,128]{3,0,2,1:T(8,128)(2,1)S(1)}, u32[]{:S(2)}, u32[]{:S(2)}) collective-permute-start(bf16[64,1,8,128]{3,0,2,1:T(8,128)(2,1)} %get-tuple-element.4), channel_id=1, source_target_pairs={{0,1},{1,2},{2,3},{3,0},{4,5},{5,6},{6,7},{7,4},{8,9},{9,10},{10,1... | collective-permute-start | bytes 393224 | tf_op jit(solution)/shard_map/ppermute | solution.py:21
  58.9 0.0 collective-permute-done
  58.9 0.3 collective-permute-done.1
  59.3 11.7 %collective-permute-done.2 = bf16[64,1,8,128]{3,0,2,1:T(8,128)(2,1)S(1)} collective-permute-done((bf16[64,1,8,128]{3,0,2,1:T(8,128)(2,1)}, bf16[64,1,8,128]{3,0,2,1:T(8,128)(2,1)S(1)}, u32[]{:S(2)}, u32[]{:S(2)}) %collective-permute-start.2) | collective-permute-done | bytes 131104 | tf_op jit(solution)/shard_map/ppermute | solution.py:21
  71.2 1.9 %all-to-all-done = bf16[64,4,8,128]{3,0,2,1:T(8,128)(2,1)S(1)} async-done(((bf16[64,4,8,128]{3,0,2,1:T(8,128)(2,1)}), bf16[64,4,8,128]{3,0,2,1:T(8,128)(2,1)S(1)}, u32[]{:S(2)}, u32[]{:S(2)}) %all-to-all-start) | async-done | bytes 524320 | tf_op jit(solution)/shard_map/all_to_all | solution.py:114
  73.2 0.3 convolution_bitcast_fusion.3
  73.5 1.0 copy.99
  74.5 0.0 all-gather.7.cloned.1.call-update
  74.6 0.4 select_convert_fusion.1
  75.0 1.4 convolution_bitcast_fusion.2
  76.4 1.9 %multiply_reduce_fusion.1 = bf16[8,128,128]{2,1,0:T(8,128)(2,1)S(1)} fusion(f32[4,8,128,128]{3,2,1,0:T(8,128)} %bitcast.127, f32[4]{0:T(128)S(1)} %compare_convert_fusion.1), kind=kLoop, calls=%fused_computation.2 | loop fusion | flops 917504 | bytes 2359312 | tf_op jit(solution)/shard_map/reduce_sum | solution.py:72
  78.4 0.3 fusion.8
  78.7 1.1 copy.90
  79.8 4.3 %all-to-all-start.3 = ((bf16[256,1,8,128]{3,2,1,0:T(8,128)(2,1)}), bf16[256,1,8,128]{3,2,1,0:T(8,128)(2,1)S(1)}, u32[]{:S(2)}, u32[]{:S(2)}) async-start(bf16[256,1,8,128]{3,2,1,0:T(8,128)(2,1)} %copy.90), calls=%async_computation.3 | async-start | bytes 1048576 | tf_op jit(solution)/shard_map/all_to_all | solution.py:106
  84.1 1.6 select_convert_fusion
  85.7 0.4 convolution_bitcast_fusion.1
  86.2 0.3 fusion.10
  86.5 0.2 copy-done
  86.7 1.1 copy.95
  87.8 11.0 %all-to-all-done.3 = bf16[256,1,8,128]{3,2,1,0:T(8,128)(2,1)S(1)} async-done(((bf16[256,1,8,128]{3,2,1,0:T(8,128)(2,1)}), bf16[256,1,8,128]{3,2,1,0:T(8,128)(2,1)S(1)}, u32[]{:S(2)}, u32[]{:S(2)}) %all-to-all-start.3) | async-done | bytes 524320 | tf_op jit(solution)/shard_map/all_to_all | solution.py:106
  98.8 4.2 %all-to-all-start.4 = ((bf16[256,1,8,128]{3,2,1,0:T(8,128)(2,1)}), bf16[256,1,8,128]{3,2,1,0:T(8,128)(2,1)}, u32[]{:S(2)}, u32[]{:S(2)}) async-start(bf16[256,1,8,128]{3,2,1,0:T(8,128)(2,1)} %copy.95), calls=%async_computation.4 | async-start | bytes 1048576 | tf_op jit(solution)/shard_map/all_to_all | solution.py:107
  103.0 2.7 %convolution_bitcast_fusion = f32[8,128,256]{1,2,0:T(8,128)} fusion(bf16[8,256,256]{2,1,0:T(8,128)(2,1)} %copy-done, bf16[256,8,128]{2,0,1:T(8,128)(2,1)S(1)} %bitcast.126), kind=kOutput, calls=%fused_computation.12 | convolution fusion | flops 134217728 | bytes 2621440 | tf_op jit(solution)/shard_map/bhts,bthd->bshd/dot_general | solution.py:91
  105.6 1.9 %multiply_reduce_fusion = bf16[8,128,128]{2,1,0:T(8,128)(2,1)S(1)} fusion(f32[4,8,128,128]{3,2,1,0:T(8,128)} %bitcast.128, f32[4]{0:T(128)S(1)} %compare_convert_fusion), kind=kLoop, calls=%fused_computation | loop fusion | flops 917504 | bytes 2359312 | tf_op jit(solution)/shard_map/reduce_sum | solution.py:73
  107.6 0.3 fusion.9
  107.9 1.1 copy.101
  109.0 8.0 %all-to-all-done.4 = bf16[256,1,8,128]{3,2,1,0:T(8,128)(2,1)} async-done(((bf16[256,1,8,128]{3,2,1,0:T(8,128)(2,1)}), bf16[256,1,8,128]{3,2,1,0:T(8,128)(2,1)}, u32[]{:S(2)}, u32[]{:S(2)}) %all-to-all-start.4) | async-done | bytes 524320 | tf_op jit(solution)/shard_map/all_to_all | solution.py:107
  117.0 3.5 %all-to-all-start.5 = ((bf16[256,1,8,128]{3,2,1,0:T(8,128)(2,1)}), bf16[256,1,8,128]{3,2,1,0:T(8,128)(2,1)S(1)}, u32[]{:S(2)}, u32[]{:S(2)}) async-start(bf16[256,1,8,128]{3,2,1,0:T(8,128)(2,1)} %copy.101), calls=%async_computation.5 | async-start | bytes 1048576 | tf_op jit(solution)/shard_map/all_to_all | solution.py:108
  120.5 0.3 convolution_multiply_fusion
  120.8 1.6 fusion.7
  122.4 1.1 copy.107
  123.5 11.0 %all-to-all-done.5 = bf16[256,1,8,128]{3,2,1,0:T(8,128)(2,1)S(1)} async-done(((bf16[256,1,8,128]{3,2,1,0:T(8,128)(2,1)}), bf16[256,1,8,128]{3,2,1,0:T(8,128)(2,1)S(1)}, u32[]{:S(2)}, u32[]{:S(2)}) %all-to-all-start.5) | async-done | bytes 524320 | tf_op jit(solution)/shard_map/all_to_all | solution.py:108
  134.5 3.5 %all-to-all-start.6 = ((bf16[256,1,8,128]{3,2,1,0:T(8,128)(2,1)}), bf16[256,1,8,128]{3,2,1,0:T(8,128)(2,1)S(1)}, u32[]{:S(2)}, u32[]{:S(2)}) async-start(bf16[256,1,8,128]{3,2,1,0:T(8,128)(2,1)} %copy.107), calls=%async_computation.6 | async-start | bytes 1048576 | tf_op jit(solution)/shard_map/all_to_all | solution.py:109
  137.9 0.1 copy.91
  138.0 1.0 reshape.186
  139.1 1.1 copy.96
  140.2 1.0 reshape.190
  141.2 0.1 copy.102
  141.3 1.0 reshape.192
  142.3 9.6 %all-to-all-done.6 = bf16[256,1,8,128]{3,2,1,0:T(8,128)(2,1)S(1)} async-done(((bf16[256,1,8,128]{3,2,1,0:T(8,128)(2,1)}), bf16[256,1,8,128]{3,2,1,0:T(8,128)(2,1)S(1)}, u32[]{:S(2)}, u32[]{:S(2)}) %all-to-all-start.6) | async-done | bytes 524320 | tf_op jit(solution)/shard_map/all_to_all | solution.py:109
  151.9 0.1 copy.108
  152.0 1.0 reshape.194
  (29 shorter events, 0.3 us)
Async XLA Ops:
  7.2 8.5 %copy-start.5 = (bf16[64,4096]{1,0:T(8,128)(2,1)S(1)}, bf16[64,4096]{1,0:T(8,128)(2,1)}, u32[]{:S(2)}) copy-start(bf16[64,4096]{1,0:T(8,128)(2,1)} %param.6) | copy-start | bytes 1572868
  9.4 20.8 %all-to-all-start.1 = ((bf16[64,4,8,128]{3,0,2,1:T(8,128)(2,1)}), bf16[64,4,8,128]{3,0,2,1:T(8,128)(2,1)S(1)}, u32[]{:S(2)}, u32[]{:S(2)}) async-start(bf16[64,4,8,128]{3,0,2,1:T(8,128)(2,1)} %copy.83), calls=%async_computation.1 | async-start | bytes 1048576 | tf_op jit(solution)/shard_map/all_to_all | solution.py:115
  30.2 17.4 %all-to-all-start.2 = ((bf16[64,4,8,128]{3,0,2,1:T(8,128)(2,1)}), bf16[64,4,8,128]{3,0,2,1:T(8,128)(2,1)S(1)}, u32[]{:S(2)}, u32[]{:S(2)}) async-start(bf16[64,4,8,128]{3,0,2,1:T(8,128)(2,1)} %copy.85), calls=%async_computation.2 | async-start | bytes 1048576 | tf_op jit(solution)/shard_map/all_to_all | solution.py:116
  33.7 42.8 %all-gather.5.cloned.1.call-start = ((), (), s32[]{:S(2)}) async-start(), calls=%async_computation.7 | async-start | bytes 2621440 | tf_op jit(solution)/shard_map/all_gather | solution.py:65
  33.7 15.2 %copy-start.6 = (bf16[64,4096]{1,0:T(8,128)(2,1)S(1)}, bf16[64,4096]{1,0:T(8,128)(2,1)}, u32[]{:S(2)}) copy-start(bf16[64,4096]{1,0:T(8,128)(2,1)} %param.7) | copy-start | bytes 1572868
  48.8 2.8 %copy-start.7 = (bf16[64,4096]{1,0:T(8,128)(2,1)S(1)}, bf16[64,4096]{1,0:T(8,128)(2,1)}, u32[]{:S(2)}) copy-start(bf16[64,4096]{1,0:T(8,128)(2,1)} %param.4) | copy-start | bytes 1572868
  50.1 8.8 %collective-permute-start = (bf16[64,1,8,128]{3,0,2,1:T(8,128)(2,1)S(1)}, bf16[64,1,8,128]{3,0,2,1:T(8,128)(2,1)S(1)}, u32[]{:S(2)}, u32[]{:S(2)}) collective-permute-start(bf16[64,1,8,128]{3,0,2,1:T(8,128)(2,1)S(1)} %get-tuple-element.6), channel_id=1, source_target_pairs={{0,3},{1,0},{2,1},{3,2},{4,7},{5,4},{6,5},{7,6},{8,11},{9,8},{10,9... | collective-permute-start | bytes 393224 | tf_op jit(solution)/shard_map/ppermute | solution.py:21
  51.6 7.7 %collective-permute-start.1 = (bf16[64,1,8,128]{3,0,2,1:T(8,128)(2,1)}, bf16[64,1,8,128]{3,0,2,1:T(8,128)(2,1)S(1)}, u32[]{:S(2)}, u32[]{:S(2)}) collective-permute-start(bf16[64,1,8,128]{3,0,2,1:T(8,128)(2,1)} %get-tuple-element.5), channel_id=1, source_target_pairs={{0,2},{1,3},{2,0},{3,1},{4,6},{5,7},{6,4},{7,5},{8,10},{9,11},{10,... | collective-permute-start | bytes 393224 | tf_op jit(solution)/shard_map/ppermute | solution.py:21
  52.7 20.4 %all-to-all-start = ((bf16[64,4,8,128]{3,0,2,1:T(8,128)(2,1)}), bf16[64,4,8,128]{3,0,2,1:T(8,128)(2,1)S(1)}, u32[]{:S(2)}, u32[]{:S(2)}) async-start(bf16[64,4,8,128]{3,0,2,1:T(8,128)(2,1)} %copy.81), calls=%async_computation | async-start | bytes 1048576 | tf_op jit(solution)/shard_map/all_to_all | solution.py:114
  56.9 48.7 %all-gather.7.cloned.1.call-start = ((), (), s32[]{:S(2)}) async-start(), calls=%async_computation.8 | async-start | bytes 2621440 | tf_op jit(solution)/shard_map/all_gather | solution.py:66
  56.9 14.1 %collective-permute-start.2 = (bf16[64,1,8,128]{3,0,2,1:T(8,128)(2,1)}, bf16[64,1,8,128]{3,0,2,1:T(8,128)(2,1)S(1)}, u32[]{:S(2)}, u32[]{:S(2)}) collective-permute-start(bf16[64,1,8,128]{3,0,2,1:T(8,128)(2,1)} %get-tuple-element.4), channel_id=1, source_target_pairs={{0,1},{1,2},{2,3},{3,0},{4,5},{5,6},{6,7},{7,4},{8,9},{9,10},{10,1... | collective-permute-start | bytes 393224 | tf_op jit(solution)/shard_map/ppermute | solution.py:21
  71.2 3.4 %copy-start.3 = (bf16[512,1,8,128]{3,0,2,1:T(8,128)(2,1)}, bf16[512,1,8,128]{3,0,2,1:T(8,128)(2,1)S(1)}, u32[]{:S(2)}) copy-start(bf16[512,1,8,128]{3,0,2,1:T(8,128)(2,1)S(1)} %slice_dynamic-update-slice_fusion.1) | copy-start | bytes 3145732
  76.4 1.9 %copy-start.2 = (f32[8,128,256]{1,2,0:T(8,128)S(1)}, f32[8,128,256]{1,2,0:T(8,128)}, u32[]{:S(2)}) copy-start(f32[8,128,256]{1,2,0:T(8,128)} %convolution_bitcast_fusion.2) | copy-start | bytes 3145732
  79.8 19.0 %all-to-all-start.3 = ((bf16[256,1,8,128]{3,2,1,0:T(8,128)(2,1)}), bf16[256,1,8,128]{3,2,1,0:T(8,128)(2,1)S(1)}, u32[]{:S(2)}, u32[]{:S(2)}) async-start(bf16[256,1,8,128]{3,2,1,0:T(8,128)(2,1)} %copy.90), calls=%async_computation.3 | async-start | bytes 1048576 | tf_op jit(solution)/shard_map/all_to_all | solution.py:106
  84.1 2.0 %copy-start.4 = (bf16[512,1,8,128]{3,0,2,1:T(8,128)(2,1)S(1)}, bf16[512,1,8,128]{3,0,2,1:T(8,128)(2,1)}, u32[]{:S(2)}) copy-start(bf16[512,1,8,128]{3,0,2,1:T(8,128)(2,1)} %copy-done.3) | copy-start | bytes 3145732
  85.7 1.0 copy-start
  98.8 18.2 %all-to-all-start.4 = ((bf16[256,1,8,128]{3,2,1,0:T(8,128)(2,1)}), bf16[256,1,8,128]{3,2,1,0:T(8,128)(2,1)}, u32[]{:S(2)}, u32[]{:S(2)}) async-start(bf16[256,1,8,128]{3,2,1,0:T(8,128)(2,1)} %copy.95), calls=%async_computation.4 | async-start | bytes 1048576 | tf_op jit(solution)/shard_map/all_to_all | solution.py:107
  105.6 1.9 %copy-start.1 = (f32[8,128,256]{1,2,0:T(8,128)S(1)}, f32[8,128,256]{1,2,0:T(8,128)}, u32[]{:S(2)}) copy-start(f32[8,128,256]{1,2,0:T(8,128)} %convolution_bitcast_fusion) | copy-start | bytes 3145732
  117.0 17.4 %all-to-all-start.5 = ((bf16[256,1,8,128]{3,2,1,0:T(8,128)(2,1)}), bf16[256,1,8,128]{3,2,1,0:T(8,128)(2,1)S(1)}, u32[]{:S(2)}, u32[]{:S(2)}) async-start(bf16[256,1,8,128]{3,2,1,0:T(8,128)(2,1)} %copy.101), calls=%async_computation.5 | async-start | bytes 1048576 | tf_op jit(solution)/shard_map/all_to_all | solution.py:108
  134.5 17.4 %all-to-all-start.6 = ((bf16[256,1,8,128]{3,2,1,0:T(8,128)(2,1)}), bf16[256,1,8,128]{3,2,1,0:T(8,128)(2,1)S(1)}, u32[]{:S(2)}, u32[]{:S(2)}) async-start(bf16[256,1,8,128]{3,2,1,0:T(8,128)(2,1)} %copy.107), calls=%async_computation.6 | async-start | bytes 1048576 | tf_op jit(solution)/shard_map/all_to_all | solution.py:109
Sparse Core Ops, SparseCore 0:
  49.0 21.6 all-gather.4
  74.7 23.2 all-gather.6
